TPU v7x, 256 devices: a whole 4x4x8 slice. The times are simulated.
256 devices in a mesh: row: 2 (over x_hi), circ: 64 (over y, z, x_lo), rad: 2 (over core).
Axes of the slice: x: 4 (x_hi: 2, x_lo: 2; x = x_hi * 2 + x_lo), y: 4, z: 8, core: 2. Of those that a mesh axis runs over, the one named last changes fastest.
Arguments:
- state: float32 [2, 5, 8, 64, 8192], P('row', None, None, 'rad', 'circ'), as said below
- inv_volume: float32 [2, 8, 64, 8192], P('row', None, 'rad', 'circ'), may hold values from 0.5 to 2
- wheel_speed: float32 [64], P('rad'), may hold values from 0.2 to 0.6
- offset: int32 [1], replicated, may hold values from 0 to 8191
Outputs:
- new_state: float32 [2, 5, 8, 64, 8192], P('row', None, None, 'rad', 'circ')
- rate: float32 [2, 5, 8, 64, 8192], P('row', None, None, 'rad', 'circ')
Inputs may be any that keep to these rules, and one draw needn't show every extreme that they name: `state`: density and pressure lie between 0.7 and 1.4, each velocity component within 0.9 in magnitude.
All inputs are finite; a program needn't handle non-finite values.
Results may differ from a plain program's by a relative error of at most 0.00002.
Values sent between devices are 32-bit elements; how exact they have to be, the bound alone decides.
A program may use at most 64 MiB of HBM per device.

v0:
```python
import functools

import jax
import jax.numpy as jnp
from jax import lax
from jax.experimental import pallas as pl
from jax.experimental.pallas import tpu as pltpu
from jax.sharding import PartitionSpec as P

GAMMA = 1.4
TIME_STEP = 0.05
MESH = pl.DeviceIdType.MESH

V1, V2, V3, PRESSURE, SOUND = 5, 6, 7, 8, 9
QUANTITIES = 10
AXIAL = (0, 1, 2, 3, 4, V1, PRESSURE, SOUND)
RADIAL = (0, 1, 2, 3, 4, V2, PRESSURE, SOUND)
CIRCUM = (0, 1, 2, 3, 4, V3, PRESSURE, SOUND)
PAD = 8
GHOST, OTHER, BEYOND, FACING = 8, 9, 10, 11
SLOTS = 16


def quantities(u):
    inverse = 1.0 / u[0]
    v1, v2, v3 = u[1] * inverse, u[2] * inverse, u[3] * inverse
    pressure = (GAMMA - 1.0) * (u[4] - 0.5 * (u[1] * v1 + u[2] * v2 + u[3] * v3))
    return list(u) + [v1, v2, v3, pressure, jnp.sqrt(GAMMA * pressure * inverse)]


def flux(cell, component):
    speed, pressure = cell[5], cell[6]
    out = [cell[c] * speed for c in range(4)] + [(cell[4] + pressure) * speed]
    out[component] = out[component] + pressure
    return out


def add_side(total, here, there, component, sign):
    wave = jnp.maximum(jnp.abs(here[5]) + here[7], jnp.abs(there[5]) + there[7])
    moved = flux(there, component)
    for c in range(5):
        term = wave * (there[c] - here[c])
        term = term - moved[c] if sign > 0 else term + moved[c]
        total[c] = term if total[c] is None else total[c] + term


def far_kernel(shift, sectors, state_ref, volume_ref, got_ref, send_sem, recv_sem):
    row = lax.axis_index("row")
    sector = lax.axis_index("circ")
    layers = state_ref.shape[2]
    near = lax.rem(sector + jnp.where(row == 0, shift, sectors - shift), sectors)
    after = lax.rem(near + jnp.where(row == 0, 1, sectors - 1), sectors)
    targets = [{"row": 1 - row, "circ": near}, {"row": 1 - row, "circ": after}]
    barrier = pltpu.get_barrier_semaphore()
    for target in targets:
        pl.semaphore_signal(barrier, inc=1, device_id=target, device_id_type=MESH)
    pl.semaphore_wait(barrier, 2)
    outer = jnp.where(row == 0, layers - 1, 0)
    inner = jnp.where(row == 0, layers - 2, 1)
    copies = []
    for j, (src, at) in enumerate(
        (
            (state_ref.at[0, :, outer], pl.ds(0, 5)),
            (state_ref.at[0, :, inner], pl.ds(5, 5)),
            (volume_ref.at[:, outer], pl.ds(10, 1)),
        )
    ):
        for i in range(2):
            copies.append(
                pltpu.make_async_remote_copy(
                    src_ref=src,
                    dst_ref=got_ref.at[i, at],
                    send_sem=send_sem.at[j, i],
                    recv_sem=recv_sem.at[j, i],
                    device_id=targets[i],
                    device_id_type=MESH,
                )
            )
    for copy in copies:
        copy.start()
    for copy in copies:
        copy.wait()


def kernel(
    sectors,
    offset_ref,
    wheel_ref,
    state_ref,
    volume_ref,
    far_ref,
    new_ref,
    rate_ref,
    cells0,
    cells1,
    volumes,
    packed,
    ghosts,
    edges,
    rows,
    send_sem,
    recv_sem,
):
    row = lax.axis_index("row")
    sector = lax.axis_index("circ")
    rad = lax.axis_index("rad")
    layers, height, width = state_ref.shape[2:]
    left = {"circ": lax.rem(sector + sectors - 1, sectors)}
    right = {"circ": lax.rem(sector + 1, sectors)}
    beside = {"rad": 1 - rad}
    barrier = pltpu.get_barrier_semaphore()
    for device in (left, right, beside):
        pl.semaphore_signal(barrier, inc=1, device_id=device, device_id_type=MESH)

    sigma = (1 - 2 * row).astype(jnp.float32)
    face_layer = jnp.where(row == 0, layers - 1, 0)
    lanes = lax.broadcasted_iota(jnp.int32, (height, width), 1)
    inner_row = PAD + jnp.where(rad == 0, height - 1, 0)
    inner_pad = PAD + jnp.where(rad == 0, height, -1)
    wall_row = PAD + jnp.where(rad == 0, 0, height - 1)
    wall_pad = PAD + jnp.where(rad == 0, -1, height)
    diagonal = lax.broadcasted_iota(jnp.int32, (height, height), 0) == lax.broadcasted_iota(
        jnp.int32, (height, height), 1
    )
    wheel = jnp.sum(
        jnp.where(diagonal, jnp.broadcast_to(wheel_ref[...], (height, height)), 0.0),
        axis=1,
        keepdims=True,
    )
    rest = lax.rem(offset_ref[0], width)
    turn = jnp.where(row == 0, lax.rem(width - rest, width), rest)
    low_lanes = lanes < jnp.where(row == 0, width - rest, rest)
    body = pl.ds(PAD, height)

    def other_frame(u, speed):
        return [
            u[0],
            u[1],
            u[2],
            u[3] + u[0] * speed,
            u[4] + u[3] * speed + 0.5 * u[0] * speed * speed,
        ]

    def window(c):
        return jnp.where(
            low_lanes,
            pltpu.roll(far_ref[row, c], turn, 1),
            pltpu.roll(far_ref[1 - row, c], turn, 1),
        )

    def keep(cells, a, u):
        values = quantities(u)
        for q in range(QUANTITIES):
            cells[q, a, body, :] = values[q]
        return values

    def pack(round_, a, values):
        first = jnp.zeros((height, width), jnp.float32)
        last = first
        for i, q in enumerate(CIRCUM):
            here = lanes == SLOTS * i
            x = values[q]
            first = jnp.where(here, pltpu.roll(x, SLOTS * i, 1) if i else x, first)
            last = jnp.where(here, pltpu.roll(x, SLOTS * i + 1, 1), last)
        here = lax.rem(lanes, SLOTS) == a
        for side, tile in ((0, first), (1, last)):
            packed[round_, side] = jnp.where(here, pltpu.roll(tile, a, 1), packed[round_, side])

    def keep_rows(cells, round_, a):
        for i, q in enumerate(RADIAL):
            rows[round_, i, pl.ds(a, 1), :] = cells[q, a, pl.ds(inner_row, 1), :]
            wall = cells[q, a, pl.ds(wall_row, 1), :]
            cells[q, a, pl.ds(wall_pad, 1), :] = -wall if q in (2, V2) else wall

    def rate_of(cells, round_, i):
        a = jnp.where(i == layers, OTHER, i)
        below = jnp.where(row == 0, jnp.maximum(i - 1, 0), jnp.where(i == 0, GHOST, i - 1))
        below = jnp.where(i == layers, jnp.where(row == 0, FACING, BEYOND), below)
        above = jnp.where(row == 0, i + 1, jnp.minimum(i + 1, layers - 1))
        above = jnp.where(i == layers, jnp.where(row == 0, BEYOND, FACING), above)
        for j, q in enumerate(RADIAL):
            cells[q, a, pl.ds(inner_pad, 1), :] = edges[round_, j, pl.ds(a, 1), :]

        def layer(qs, slot, by=0):
            return [cells[q, slot, pl.ds(PAD + by, height), :] for q in qs]

        total = [None] * 5
        here = layer(AXIAL, a)
        add_side(total, here, layer(AXIAL, above), 1, 1)
        add_side(total, here, layer(AXIAL, below), 1, -1)
        here = layer(RADIAL, a)
        add_side(total, here, layer(RADIAL, a, 1), 2, 1)
        add_side(total, here, layer(RADIAL, a, -1), 2, -1)
        here = layer(CIRCUM, a)
        before = pltpu.roll(ghosts[round_, 0], lax.rem(width - a, width), 1)
        after = pltpu.roll(ghosts[round_, 1], width - 1 - a, 1)
        up, down = [], []
        for j in range(8):
            ghost = pltpu.roll(after, width - SLOTS * j, 1) if j else after
            up.append(jnp.where(lanes == width - 1, ghost, pltpu.roll(here[j], width - 1, 1)))
            ghost = pltpu.roll(before, width - SLOTS * j, 1) if j else before
            down.append(jnp.where(lanes == 0, ghost, pltpu.roll(here[j], 1, 1)))
        add_side(total, here, up, 3, 1)
        add_side(total, here, down, 3, -1)
        half = 0.5 * volumes[i]
        return a, [half * part for part in total]

    def local_copies(round_):
        return [
            pltpu.make_async_remote_copy(
                src_ref=src,
                dst_ref=dst,
                send_sem=send_sem.at[round_, i],
                recv_sem=recv_sem.at[round_, i],
                device_id=device,
                device_id_type=MESH,
            )
            for i, (src, dst, device) in enumerate(
                (
                    (packed.at[round_, 0], ghosts.at[round_, 1], left),
                    (packed.at[round_, 1], ghosts.at[round_, 0], right),
                    (rows.at[round_], edges.at[round_], beside),
                )
            )
        ]

    def send(copies):
        for copy in copies:
            copy.start()
        for copy in copies:
            copy.wait_recv()

    local = [local_copies(r) for r in range(2)]
    for r in range(2):
        packed[r] = jnp.zeros_like(packed[r])
        rows[r] = jnp.zeros_like(rows[r])

    def prepare(a, carry):
        pack(0, a, keep(cells0, a, [state_ref[0, c, a] for c in range(5)]))
        keep_rows(cells0, 0, a)
        volumes[a] = volume_ref[0, a]
        return carry

    lax.fori_loop(0, layers, prepare, 0)
    other = [window(c) for c in range(5)]
    pack(0, OTHER, keep(cells0, OTHER, other))
    keep_rows(cells0, 0, OTHER)
    keep(cells0, GHOST, other_frame(other, -sigma * wheel))
    volumes[layers] = window(10)

    pl.semaphore_wait(barrier, 3)
    for copy in local[0]:
        copy.start()
    keep(cells0, BEYOND, [window(5 + c) for c in range(5)])
    mine = [state_ref[0, c, face_layer] for c in range(5)]
    keep(cells0, FACING, other_frame(mine, sigma * wheel))
    for copy in local[0]:
        copy.wait_recv()

    def first_section(i, carry):
        a, rate = rate_of(cells0, 0, i)
        u = [cells0[c, a, body, :] + TIME_STEP * rate[c] for c in range(5)]
        turned = jnp.where(i == layers, -sigma, 0.0) * wheel
        pack(1, i, keep(cells1, i, other_frame(u, turned)))
        keep_rows(cells1, 1, i)
        return carry

    lax.fori_loop(0, layers + 1, first_section, 0)
    send(local[1])

    def second_section(i, carry):
        _, rate = rate_of(cells1, 1, i)
        for c in range(5):
            rate_ref[0, c, i] = rate[c]
            new_ref[0, c, i] = 0.5 * cells0[c, i, body, :] + 0.5 * (
                cells1[c, i, body, :] + TIME_STEP * rate[c]
            )
        return carry

    lax.fori_loop(0, layers, second_section, 0)
    for copy in local[0] + local[1]:
        copy.wait_send()


def far(shift, state, inv_volume):
    height, width = state.shape[3:]
    anywhere = pl.BlockSpec(memory_space=pl.ANY)
    return pl.pallas_call(
        functools.partial(far_kernel, shift, lax.axis_size("circ")),
        out_shape=jax.ShapeDtypeStruct((2, 11, height, width), jnp.float32),
        in_specs=[anywhere, anywhere],
        out_specs=anywhere,
        scratch_shapes=[pltpu.SemaphoreType.DMA((3, 2)), pltpu.SemaphoreType.DMA((3, 2))],
        compiler_params=pltpu.CompilerParams(collective_id=shift, has_side_effects=True),
    )(state, inv_volume)


def on_device(state, inv_volume, wheel_speed, offset):
    sectors = lax.axis_size("circ")
    layers, height, width = state.shape[2:]
    arrived = lax.switch(
        offset[0] // width,
        [functools.partial(far, shift) for shift in range(sectors)],
        state,
        inv_volume,
    )
    f32 = jnp.float32
    cells = pltpu.VMEM((QUANTITIES, layers + 4, height + 2 * PAD, width), f32)
    vmem = pl.BlockSpec(memory_space=pltpu.VMEM)
    out = jax.ShapeDtypeStruct(state.shape, f32)
    return pl.pallas_call(
        functools.partial(kernel, sectors),
        out_shape=(out, out),
        in_specs=[pl.BlockSpec(memory_space=pltpu.SMEM)] + [vmem] * 4,
        out_specs=(vmem, vmem),
        scratch_shapes=[
            cells,
            cells,
            pltpu.VMEM((layers + 1, height, width), f32),
            pltpu.VMEM((2, 2, height, width), f32),
            pltpu.VMEM((2, 2, height, width), f32),
            pltpu.VMEM((2, 8, SLOTS, width), f32),
            pltpu.VMEM((2, 8, SLOTS, width), f32),
            pltpu.SemaphoreType.DMA((2, 3)),
            pltpu.SemaphoreType.DMA((2, 3)),
        ],
        compiler_params=pltpu.CompilerParams(
            collective_id=sectors, has_side_effects=True, vmem_limit_bytes=32 * 2**20
        ),
    )(offset, wheel_speed[None, :], state, inv_volume, arrived)


def solution(mesh):
    return jax.shard_map(
        on_device,
        mesh=mesh,
        in_specs=(
            P("row", None, None, "rad", "circ"),
            P("row", None, "rad", "circ"),
            P("rad"),
            P(),
        ),
        out_specs=(P("row", None, None, "rad", "circ"), P("row", None, None, "rad", "circ")),
        check_vma=False,
    )
```

profile of v0, /device:TPU:4, one launch (start us, length us, event | category | flops | bytes accessed | tf_op | source)
XLA Modules:
  0.0 64.6 jit_solution(12407797630539705865)
XLA Ops:
  1.3 25.1 %conditional.1 = (f32[2,11,32,128]{3,2,1,0:T(8,128)S(1)}) conditional(s32[]{:T(128)} %clamp.3, (f32[1,5,8,32,128]{4,3,2,1,0:T(8,128)}, f32[1,8,32,128]{3,2,1,0:T(8,128)}) %tuple.199, (f32[1,5,8,32,128]{4,3,2,1,0:T(8,128)}, f32[1,8,32,128]{3,2,1,0:T(8,128)}) %tuple.199, (f32[1,5,8,32,128]{4,3,2,1,0:T(8,128)}, ...), branch_computations={%region_0.1_spmd, %region_1.2_spmd, %region_2.3_spmd, %region_3.4_... | conditional | bytes 8 | solution.py:301
  1.4 24.8 %branch_19_fun.1 = f32[2,11,32,128]{3,2,1,0:T(8,128)S(1)} custom-call(f32[1,5,8,32,128]{4,3,2,1,0:T(8,128)} %get-tuple-element.332.state_ref, f32[1,8,32,128]{3,2,1,0:T(8,128)} %get-tuple-element.336.volume_ref), custom_call_target="tpu_custom_call" | custom-call | tf_op jit(solution)/shard_map/cond/branch_19_fun/pallas_call | solution.py:288
  26.4 0.0 copy-start
  26.4 0.6 %copy-done = f32[32]{0:T(128)S(1)} copy-done((f32[32]{0:T(128)S(1)}, f32[32]{0:T(128)}, u32[]{:S(2)}) %copy-start) | copy-done | bytes 152
  27.1 35.9 %shard_map.59 = (f32[1,5,8,32,128]{4,3,2,1,0:T(8,128)S(1)}, f32[1,5,8,32,128]{4,3,2,1,0:T(8,128)S(1)}) custom-call(s32[1]{0:T(128)} %copy.72.offset_ref, f32[1,32]{1,0:T(1,128)S(1)} %bitcast.6, f32[1,5,8,32,128]{4,3,2,1,0:T(8,128)} %state_ref.1, f32[1,8,32,128]{3,2,1,0:T(8,128)} %volume_ref.1, f32[2,11,32,128]{3,2,1,0:T(8,128)S(1)} %get-tuple-element.455.far_ref), custom_call_target="tpu_custom_call" | custom-call | tf_op jit(solution)/shard_map/pallas_call | solution.py:311
  62.9 0.8 %copy.73 = f32[1,5,8,32,128]{4,3,2,1,0:T(8,128)} copy(f32[1,5,8,32,128]{4,3,2,1,0:T(8,128)S(1)} %get-tuple-element.453) | data formatting | bytes 1310720
  63.8 0.8 %copy.74 = f32[1,5,8,32,128]{4,3,2,1,0:T(8,128)} copy(f32[1,5,8,32,128]{4,3,2,1,0:T(8,128)S(1)} %get-tuple-element.454) | data formatting | bytes 1310720
Async XLA Ops:
  26.4 0.7 %copy-start = (f32[32]{0:T(128)S(1)}, f32[32]{0:T(128)}, u32[]{:S(2)}) copy-start(f32[32]{0:T(128)} %param.70) | copy-start | bytes 388
where the time goes:
time: 64.7 us; the launch traced here: 64.6 us
  Pallas kernels  60.7 us (94%)
  local copies, waits for them, and re-layouts  2.33 us (4%)
  between operations  1.32 us (2%)
    pallas_call x1, Pallas kernels, on_device(): pl.pallas_call(functools.partial(kernel, sectors), out_shape=(out, out),...  35.9 us
    pallas_call x1, Pallas kernels, far(): pl.pallas_call(functools.partial(far_kernel, shift, lax.axis_size('circ')...  24.8 us
    unnamed x4, local copies, waits for them, and re-layouts  2.33 us

commit v1 on v0

--- a/solution.py
+++ b/solution.py
@@ -18,6 +18,7 @@
 CIRCUM = (0, 1, 2, 3, 4, V3, PRESSURE, SOUND)
 PAD = 8
 GHOST, OTHER, BEYOND, FACING = 8, 9, 10, 11
+SPARE = 12
 SLOTS = 16
 
 
@@ -49,12 +50,10 @@
     sector = lax.axis_index("circ")
     layers = state_ref.shape[2]
     near = lax.rem(sector + jnp.where(row == 0, shift, sectors - shift), sectors)
-    after = lax.rem(near + jnp.where(row == 0, 1, sectors - 1), sectors)
-    targets = [{"row": 1 - row, "circ": near}, {"row": 1 - row, "circ": after}]
+    target = {"row": 1 - row, "circ": near}
     barrier = pltpu.get_barrier_semaphore()
-    for target in targets:
-        pl.semaphore_signal(barrier, inc=1, device_id=target, device_id_type=MESH)
-    pl.semaphore_wait(barrier, 2)
+    pl.semaphore_signal(barrier, inc=1, device_id=target, device_id_type=MESH)
+    pl.semaphore_wait(barrier, 1)
     outer = jnp.where(row == 0, layers - 1, 0)
     inner = jnp.where(row == 0, layers - 2, 1)
     copies = []
@@ -65,17 +64,16 @@
             (volume_ref.at[:, outer], pl.ds(10, 1)),
         )
     ):
-        for i in range(2):
-            copies.append(
-                pltpu.make_async_remote_copy(
-                    src_ref=src,
-                    dst_ref=got_ref.at[i, at],
-                    send_sem=send_sem.at[j, i],
-                    recv_sem=recv_sem.at[j, i],
-                    device_id=targets[i],
-                    device_id_type=MESH,
-                )
+        copies.append(
+            pltpu.make_async_remote_copy(
+                src_ref=src,
+                dst_ref=got_ref.at[at],
+                send_sem=send_sem.at[j],
+                recv_sem=recv_sem.at[j],
+                device_id=target,
+                device_id_type=MESH,
             )
+        )
     for copy in copies:
         copy.start()
     for copy in copies:
@@ -98,6 +96,8 @@
     ghosts,
     edges,
     rows,
+    halves_out,
+    halves_in,
     send_sem,
     recv_sem,
 ):
@@ -127,7 +127,7 @@
         axis=1,
         keepdims=True,
     )
-    rest = lax.rem(offset_ref[0], width)
+    rest = lax.rem(offset_ref[0] + width // 2, width)
     turn = jnp.where(row == 0, lax.rem(width - rest, width), rest)
     low_lanes = lanes < jnp.where(row == 0, width - rest, rest)
     body = pl.ds(PAD, height)
@@ -141,12 +141,28 @@
             u[4] + u[3] * speed + 0.5 * u[0] * speed * speed,
         ]
 
+    half_width, half_height = width // 2, height // 2
+    low_half = lanes < half_width
+    low_top = lanes[:half_height] < half_width
+
+    def split(c):
+        top, bottom = far_ref[c, :half_height], far_ref[c, half_height:]
+        halves_out[0, c] = jnp.where(low_top, top, pltpu.roll(bottom, half_width, 1))
+        halves_out[1, c] = jnp.where(low_top, pltpu.roll(top, half_width, 1), bottom)
+
+    def turned(c):
+        middle = pltpu.roll(far_ref[c], half_width, 1)
+        late, early = halves_in[0, c], halves_in[1, c]
+        before = jnp.concatenate([early, pltpu.roll(early, half_width, 1)])
+        after = jnp.concatenate([pltpu.roll(late, half_width, 1), late])
+        return (
+            pltpu.roll(jnp.where(low_half, before, middle), turn, 1),
+            pltpu.roll(jnp.where(low_half, middle, after), turn, 1),
+        )
+
     def window(c):
-        return jnp.where(
-            low_lanes,
-            pltpu.roll(far_ref[row, c], turn, 1),
-            pltpu.roll(far_ref[1 - row, c], turn, 1),
-        )
+        low, high = turned(c)
+        return jnp.where(low_lanes, low, high)
 
     def keep(cells, a, u):
         values = quantities(u)
@@ -154,17 +170,20 @@
             cells[q, a, body, :] = values[q]
         return values
 
-    def pack(round_, a, values):
+    def columns(a, firsts, lasts):
         first = jnp.zeros((height, width), jnp.float32)
         last = first
         for i, q in enumerate(CIRCUM):
             here = lanes == SLOTS * i
-            x = values[q]
+            x = firsts[q]
             first = jnp.where(here, pltpu.roll(x, SLOTS * i, 1) if i else x, first)
-            last = jnp.where(here, pltpu.roll(x, SLOTS * i + 1, 1), last)
+            last = jnp.where(here, pltpu.roll(lasts[q], SLOTS * i + 1, 1), last)
+        return pltpu.roll(first, a, 1), pltpu.roll(last, a, 1)
+
+    def pack(round_, a, values):
         here = lax.rem(lanes, SLOTS) == a
-        for side, tile in ((0, first), (1, last)):
-            packed[round_, side] = jnp.where(here, pltpu.roll(tile, a, 1), packed[round_, side])
+        for side, tile in enumerate(columns(a, values, values)):
+            packed[round_, side] = jnp.where(here, tile, packed[round_, side])
 
     def keep_rows(cells, round_, a):
         for i, q in enumerate(RADIAL):
@@ -219,9 +238,13 @@
                 (
                     (packed.at[round_, 0], ghosts.at[round_, 1], left),
                     (packed.at[round_, 1], ghosts.at[round_, 0], right),
-                    (rows.at[round_], edges.at[round_], beside),
+                    (rows.at[round_, :, pl.ds(0, 8)], edges.at[round_, :, pl.ds(0, 8)], beside),
+                    (halves_out.at[0], halves_in.at[0], left),
+                    (halves_out.at[1], halves_in.at[1], right),
+                    (rows.at[round_, :, pl.ds(8, 8)], edges.at[round_, :, pl.ds(8, 8)], beside),
                 )
             )
+            if round_ == 0 or i < 3
         ]
 
     def send(copies):
@@ -242,22 +265,42 @@
         return carry
 
     lax.fori_loop(0, layers, prepare, 0)
-    other = [window(c) for c in range(5)]
-    pack(0, OTHER, keep(cells0, OTHER, other))
-    keep_rows(cells0, 0, OTHER)
-    keep(cells0, GHOST, other_frame(other, -sigma * wheel))
-    volumes[layers] = window(10)
+    for c in range(11):
+        split(c)
+    middle = [pltpu.roll(far_ref[c], half_width, 1) for c in range(5)]
+    pack(0, SPARE, quantities(middle))
 
     pl.semaphore_wait(barrier, 3)
-    for copy in local[0]:
+    for copy in local[0][:5]:
         copy.start()
-    keep(cells0, BEYOND, [window(5 + c) for c in range(5)])
     mine = [state_ref[0, c, face_layer] for c in range(5)]
     keep(cells0, FACING, other_frame(mine, sigma * wheel))
-    for copy in local[0]:
+    for copy in local[0][:5]:
         copy.wait_recv()
 
+    pairs = [turned(c) for c in range(5)]
+    other = [jnp.where(low_lanes, low, high) for low, high in pairs]
+    keep(cells0, OTHER, other)
+    keep_rows(cells0, 0, OTHER)
+    local[0][5].start()
+    keep(cells0, GHOST, other_frame(other, -sigma * wheel))
+    keep(cells0, BEYOND, [window(5 + c) for c in range(5)])
+    volumes[layers] = window(10)
+    late, early = columns(
+        OTHER, quantities([high for _, high in pairs]), quantities([low for low, _ in pairs])
+    )
+    begin = jnp.where(row == 0, rest, width - rest)
+    here = lax.rem(lanes, SLOTS) == OTHER
+    for side, tile, edge in ((0, early, 0), (1, late, width)):
+        got = ghosts[0, side]
+        spare = pltpu.roll(got, width + OTHER - SPARE, 1)
+        ghosts[0, side] = jnp.where(here, jnp.where(begin == edge, spare, tile), got)
+
     def first_section(i, carry):
+        @pl.when(i == layers)
+        def _():
+            local[0][5].wait_recv()
+
         a, rate = rate_of(cells0, 0, i)
         u = [cells0[c, a, body, :] + TIME_STEP * rate[c] for c in range(5)]
         turned = jnp.where(i == layers, -sigma, 0.0) * wheel
@@ -287,11 +330,11 @@
     anywhere = pl.BlockSpec(memory_space=pl.ANY)
     return pl.pallas_call(
         functools.partial(far_kernel, shift, lax.axis_size("circ")),
-        out_shape=jax.ShapeDtypeStruct((2, 11, height, width), jnp.float32),
+        out_shape=jax.ShapeDtypeStruct((11, height, width), jnp.float32),
         in_specs=[anywhere, anywhere],
         out_specs=anywhere,
-        scratch_shapes=[pltpu.SemaphoreType.DMA((3, 2)), pltpu.SemaphoreType.DMA((3, 2))],
-        compiler_params=pltpu.CompilerParams(collective_id=shift, has_side_effects=True),
+        scratch_shapes=[pltpu.SemaphoreType.DMA((3,)), pltpu.SemaphoreType.DMA((3,))],
+        compiler_params=pltpu.CompilerParams(collective_id=shift + 1, has_side_effects=True),
     )(state, inv_volume)
 
 
@@ -299,7 +342,7 @@
     sectors = lax.axis_size("circ")
     layers, height, width = state.shape[2:]
     arrived = lax.switch(
-        offset[0] // width,
+        lax.rem((offset[0] + width // 2) // width, sectors),
         [functools.partial(far, shift) for shift in range(sectors)],
         state,
         inv_volume,
@@ -321,11 +364,13 @@
             pltpu.VMEM((2, 2, height, width), f32),
             pltpu.VMEM((2, 8, SLOTS, width), f32),
             pltpu.VMEM((2, 8, SLOTS, width), f32),
-            pltpu.SemaphoreType.DMA((2, 3)),
-            pltpu.SemaphoreType.DMA((2, 3)),
+            pltpu.VMEM((2, 11, height // 2, width), f32),
+            pltpu.VMEM((2, 11, height // 2, width), f32),
+            pltpu.SemaphoreType.DMA((2, 6)),
+            pltpu.SemaphoreType.DMA((2, 6)),
         ],
         compiler_params=pltpu.CompilerParams(
-            collective_id=sectors, has_side_effects=True, vmem_limit_bytes=32 * 2**20
+            collective_id=0, has_side_effects=True, vmem_limit_bytes=32 * 2**20
         ),
     )(offset, wheel_speed[None, :], state, inv_volume, arrived)
 

time: 64.7 us -> 57.7 us (0.89)
  Pallas kernels: 60.7 us -> 53.9 us
    pallas_call x1, Pallas kernels: 35.9 us -> 23.1 us  [on_device(): pl.pallas_call(functools.partial(kernel, sectors), out_shape=(out, out),...]
    pallas_call x1, Pallas kernels: 24.8 us -> 30.7 us  [far(): pl.pallas_call(functools.partial(far_kernel, shift, lax.axis_size('circ')...]
where the time goes in v1:
time: 57.7 us; the launch traced here: 57.6 us
  Pallas kernels  53.9 us (93%)
  local copies, waits for them, and re-layouts  2.33 us (4%)
  between operations  1.33 us (2%)
    pallas_call x1, Pallas kernels, far(): pl.pallas_call(functools.partial(far_kernel, shift, lax.axis_size('circ')...  30.7 us
    pallas_call x1, Pallas kernels, on_device(): pl.pallas_call(functools.partial(kernel, sectors), out_shape=(out, out),...  23.1 us
    unnamed x4, local copies, waits for them, and re-layouts  2.33 us

profile of v1, /device:TPU:4, one launch (start us, length us, event | category | flops | bytes accessed | tf_op | source)
XLA Modules:
  0.0 57.6 jit_solution(464708819955714)
XLA Ops:
  1.3 30.8 %conditional.1 = (f32[11,32,128]{2,1,0:T(8,128)S(1)}) conditional(s32[]{:T(128)} %clamp.3, (f32[1,5,8,32,128]{4,3,2,1,0:T(8,128)}, f32[1,8,32,128]{3,2,1,0:T(8,128)}) %tuple.199, (f32[1,5,8,32,128]{4,3,2,1,0:T(8,128)}, f32[1,8,32,128]{3,2,1,0:T(8,128)}) %tuple.199, (f32[1,5,8,32,128]{4,3,2,1,0:T(8,128)}, ...), branch_computations={%region_0.1_spmd, %region_1.2_spmd, %region_2.3_spmd, %region_3.4_... | conditional | bytes 8 | solution.py:344
  1.4 30.7 %branch_53_fun.1 = f32[11,32,128]{2,1,0:T(8,128)S(1)} custom-call(f32[1,5,8,32,128]{4,3,2,1,0:T(8,128)} %get-tuple-element.427.state_ref, f32[1,8,32,128]{3,2,1,0:T(8,128)} %get-tuple-element.428.volume_ref), custom_call_target="tpu_custom_call" | custom-call | tf_op jit(solution)/shard_map/cond/branch_53_fun/pallas_call | solution.py:331
  32.1 0.0 copy-start
  32.1 0.6 %copy-done = f32[32]{0:T(128)S(1)} copy-done((f32[32]{0:T(128)S(1)}, f32[32]{0:T(128)}, u32[]{:S(2)}) %copy-start) | copy-done | bytes 152
  32.8 23.1 %shard_map.59 = (f32[1,5,8,32,128]{4,3,2,1,0:T(8,128)S(1)}, f32[1,5,8,32,128]{4,3,2,1,0:T(8,128)S(1)}) custom-call(s32[1]{0:T(128)S(6)} %copy.72.offset_ref, f32[1,32]{1,0:T(1,128)S(1)} %bitcast.2, f32[1,5,8,32,128]{4,3,2,1,0:T(8,128)} %state_ref.1, f32[1,8,32,128]{3,2,1,0:T(8,128)} %volume_ref.1, f32[11,32,128]{2,1,0:T(8,128)S(1)} %get-tuple-element.455.far_ref), custom_call_target="tpu_custom_call" | custom-call | tf_op jit(solution)/shard_map/pallas_call | solution.py:354
  55.9 0.8 %copy.73 = f32[1,5,8,32,128]{4,3,2,1,0:T(8,128)} copy(f32[1,5,8,32,128]{4,3,2,1,0:T(8,128)S(1)} %get-tuple-element.453) | data formatting | bytes 1310720
  56.8 0.8 %copy.74 = f32[1,5,8,32,128]{4,3,2,1,0:T(8,128)} copy(f32[1,5,8,32,128]{4,3,2,1,0:T(8,128)S(1)} %get-tuple-element.454) | data formatting | bytes 1310720
Async XLA Ops:
  32.1 0.7 %copy-start = (f32[32]{0:T(128)S(1)}, f32[32]{0:T(128)}, u32[]{:S(2)}) copy-start(f32[32]{0:T(128)} %param.70) | copy-start | bytes 388

commit v2 on v1

--- a/solution.py
+++ b/solution.py
@@ -17,6 +17,7 @@
 RADIAL = (0, 1, 2, 3, 4, V2, PRESSURE, SOUND)
 CIRCUM = (0, 1, 2, 3, 4, V3, PRESSURE, SOUND)
 PAD = 8
+GROUP = 8
 GHOST, OTHER, BEYOND, FACING = 8, 9, 10, 11
 SPARE = 12
 SLOTS = 16
@@ -49,11 +50,14 @@
     row = lax.axis_index("row")
     sector = lax.axis_index("circ")
     layers = state_ref.shape[2]
-    near = lax.rem(sector + jnp.where(row == 0, shift, sectors - shift), sectors)
-    target = {"row": 1 - row, "circ": near}
+    targets = []
+    for way in (shift, shift + GROUP):
+        near = lax.rem(sector + jnp.where(row == 0, way, sectors - way), sectors)
+        targets.append({"row": 1 - row, "circ": near})
     barrier = pltpu.get_barrier_semaphore()
-    pl.semaphore_signal(barrier, inc=1, device_id=target, device_id_type=MESH)
-    pl.semaphore_wait(barrier, 1)
+    for target in targets:
+        pl.semaphore_signal(barrier, inc=1, device_id=target, device_id_type=MESH)
+    pl.semaphore_wait(barrier, 2)
     outer = jnp.where(row == 0, layers - 1, 0)
     inner = jnp.where(row == 0, layers - 2, 1)
     copies = []
@@ -64,16 +68,17 @@
             (volume_ref.at[:, outer], pl.ds(10, 1)),
         )
     ):
-        copies.append(
-            pltpu.make_async_remote_copy(
-                src_ref=src,
-                dst_ref=got_ref.at[at],
-                send_sem=send_sem.at[j],
-                recv_sem=recv_sem.at[j],
-                device_id=target,
-                device_id_type=MESH,
+        for i, target in enumerate(targets):
+            copies.append(
+                pltpu.make_async_remote_copy(
+                    src_ref=src,
+                    dst_ref=got_ref.at[i, at],
+                    send_sem=send_sem.at[j, i],
+                    recv_sem=recv_sem.at[j, i],
+                    device_id=target,
+                    device_id_type=MESH,
+                )
             )
-        )
     for copy in copies:
         copy.start()
     for copy in copies:
@@ -128,6 +133,7 @@
         keepdims=True,
     )
     rest = lax.rem(offset_ref[0] + width // 2, width)
+    pick = lax.rem((offset_ref[0] + width // 2) // (width * GROUP), 2)
     turn = jnp.where(row == 0, lax.rem(width - rest, width), rest)
     low_lanes = lanes < jnp.where(row == 0, width - rest, rest)
     body = pl.ds(PAD, height)
@@ -146,12 +152,12 @@
     low_top = lanes[:half_height] < half_width
 
     def split(c):
-        top, bottom = far_ref[c, :half_height], far_ref[c, half_height:]
+        top, bottom = far_ref[pick, c, :half_height], far_ref[pick, c, half_height:]
         halves_out[0, c] = jnp.where(low_top, top, pltpu.roll(bottom, half_width, 1))
         halves_out[1, c] = jnp.where(low_top, pltpu.roll(top, half_width, 1), bottom)
 
     def turned(c):
-        middle = pltpu.roll(far_ref[c], half_width, 1)
+        middle = pltpu.roll(far_ref[pick, c], half_width, 1)
         late, early = halves_in[0, c], halves_in[1, c]
         before = jnp.concatenate([early, pltpu.roll(early, half_width, 1)])
         after = jnp.concatenate([pltpu.roll(late, half_width, 1), late])
@@ -267,7 +273,7 @@
     lax.fori_loop(0, layers, prepare, 0)
     for c in range(11):
         split(c)
-    middle = [pltpu.roll(far_ref[c], half_width, 1) for c in range(5)]
+    middle = [pltpu.roll(far_ref[pick, c], half_width, 1) for c in range(5)]
     pack(0, SPARE, quantities(middle))
 
     pl.semaphore_wait(barrier, 3)
@@ -330,20 +336,25 @@
     anywhere = pl.BlockSpec(memory_space=pl.ANY)
     return pl.pallas_call(
         functools.partial(far_kernel, shift, lax.axis_size("circ")),
-        out_shape=jax.ShapeDtypeStruct((11, height, width), jnp.float32),
+        out_shape=jax.ShapeDtypeStruct((2, 11, height, width), jnp.float32),
         in_specs=[anywhere, anywhere],
         out_specs=anywhere,
-        scratch_shapes=[pltpu.SemaphoreType.DMA((3,)), pltpu.SemaphoreType.DMA((3,))],
-        compiler_params=pltpu.CompilerParams(collective_id=shift + 1, has_side_effects=True),
+        scratch_shapes=[pltpu.SemaphoreType.DMA((3, 2)), pltpu.SemaphoreType.DMA((3, 2))],
+        compiler_params=pltpu.CompilerParams(collective_id=1 + shift // 2 // GROUP * GROUP + shift % GROUP, has_side_effects=True),
     )(state, inv_volume)
 
 
 def on_device(state, inv_volume, wheel_speed, offset):
     sectors = lax.axis_size("circ")
     layers, height, width = state.shape[2:]
+    whole = lax.rem((offset[0] + width // 2) // width, sectors)
     arrived = lax.switch(
-        lax.rem((offset[0] + width // 2) // width, sectors),
-        [functools.partial(far, shift) for shift in range(sectors)],
+        whole // (2 * GROUP) * GROUP + lax.rem(whole, GROUP),
+        [
+            functools.partial(far, first + shift)
+            for first in range(0, sectors, 2 * GROUP)
+            for shift in range(GROUP)
+        ],
         state,
         inv_volume,
     )

time: 57.7 us -> 51.3 us (0.89)
  Pallas kernels: 53.9 us -> 47.5 us
    pallas_call x1, Pallas kernels: 30.7 us -> 20.2 us  [far(): pl.pallas_call(functools.partial(far_kernel, shift, lax.axis_size('circ')...]
    pallas_call x1, Pallas kernels: 23.1 us -> 27.3 us  [on_device(): pl.pallas_call(functools.partial(kernel, sectors), out_shape=(out, out),...]
where the time goes in v2:
time: 51.3 us; the launch traced here: 51.2 us
  Pallas kernels  47.5 us (93%)
  local copies, waits for them, and re-layouts  2.33 us (5%)
  between operations  1.36 us (3%)
    pallas_call x1, Pallas kernels, on_device(): pl.pallas_call(functools.partial(kernel, sectors), out_shape=(out, out),...  27.3 us
    pallas_call x1, Pallas kernels, far(): pl.pallas_call(functools.partial(far_kernel, shift, lax.axis_size('circ')...  20.2 us
    unnamed x4, local copies, waits for them, and re-layouts  2.33 us

profile of v2, /device:TPU:4, one launch (start us, length us, event | category | flops | bytes accessed | tf_op | source)
XLA Modules:
  0.0 51.2 jit_solution(6060438163881510702)
XLA Ops:
  1.3 20.2 %conditional.1 = (f32[2,11,32,128]{3,2,1,0:T(8,128)S(1)}) conditional(s32[]{:T(128)} %clamp.3, (f32[1,5,8,32,128]{4,3,2,1,0:T(8,128)}, f32[1,8,32,128]{3,2,1,0:T(8,128)}) %tuple.103, (f32[1,5,8,32,128]{4,3,2,1,0:T(8,128)}, f32[1,8,32,128]{3,2,1,0:T(8,128)}) %tuple.103, (f32[1,5,8,32,128]{4,3,2,1,0:T(8,128)}, ...), branch_computations={%region_0.1_spmd, %region_1.2_spmd, %region_2.3_spmd, %region_3.4_... | conditional | bytes 8 | solution.py:351
  1.4 20.2 %branch_22_fun.1 = f32[2,11,32,128]{3,2,1,0:T(8,128)S(1)} custom-call(f32[1,5,8,32,128]{4,3,2,1,0:T(8,128)} %get-tuple-element.205.state_ref, f32[1,8,32,128]{3,2,1,0:T(8,128)} %get-tuple-element.206.volume_ref), custom_call_target="tpu_custom_call" | custom-call | tf_op jit(solution)/shard_map/cond/branch_22_fun/pallas_call | solution.py:337
  21.6 0.0 copy-start
  21.6 0.6 %copy-done = f32[32]{0:T(128)S(1)} copy-done((f32[32]{0:T(128)S(1)}, f32[32]{0:T(128)}, u32[]{:S(2)}) %copy-start) | copy-done | bytes 152
  22.2 27.3 %shard_map.59 = (f32[1,5,8,32,128]{4,3,2,1,0:T(8,128)S(1)}, f32[1,5,8,32,128]{4,3,2,1,0:T(8,128)S(1)}) custom-call(s32[1]{0:T(128)S(6)} %copy.40.offset_ref, f32[1,32]{1,0:T(1,128)S(1)} %bitcast.2, f32[1,5,8,32,128]{4,3,2,1,0:T(8,128)} %state_ref.1, f32[1,8,32,128]{3,2,1,0:T(8,128)} %volume_ref.1, f32[2,11,32,128]{3,2,1,0:T(8,128)S(1)} %get-tuple-element.231.far_ref), custom_call_target="tpu_custom_call" | custom-call | tf_op jit(solution)/shard_map/pallas_call | solution.py:365
  49.5 0.8 %copy.41 = f32[1,5,8,32,128]{4,3,2,1,0:T(8,128)} copy(f32[1,5,8,32,128]{4,3,2,1,0:T(8,128)S(1)} %get-tuple-element.229) | data formatting | bytes 1310720
  50.4 0.8 %copy.42 = f32[1,5,8,32,128]{4,3,2,1,0:T(8,128)} copy(f32[1,5,8,32,128]{4,3,2,1,0:T(8,128)S(1)} %get-tuple-element.230) | data formatting | bytes 1310720
Async XLA Ops:
  21.6 0.7 %copy-start = (f32[32]{0:T(128)S(1)}, f32[32]{0:T(128)}, u32[]{:S(2)}) copy-start(f32[32]{0:T(128)} %param.38) | copy-start | bytes 388
